TPU v7x, 32 devices: a whole 2x2x4 slice. The times are simulated.
32 devices in a mesh: ev: 2 (over x), sp: 16 (over z, y, core).
Axes of the slice: x: 2, y: 2, z: 4, core: 2. Of those that a mesh axis runs over, the one named last changes fastest.
Arguments:
- partial_kernels: float32 [2, 32, 32, 128], P('ev', None, 'sp'), may hold values from -6 to 6
- block_ids: int32 [2, 32], P('ev', 'sp'), may hold values from 0 to 63, as said below
- radial_smoother: float32 [128, 128], replicated, may hold values from -0.5 to 2
- shell_level: int32 [128], P('sp'), may hold values from 1 to 4
- lateral_scale: float32 [128, 256], replicated, may hold values from 0.5 to 1
Outputs:
- smoothed_kernel: float32 [128, 128, 256], P('sp', None, 'ev')
Inputs may be any that keep to these rules, and one draw needn't show every extreme that they name: `block_ids`: each index of ev and sp holds 2 distinct ids; an id's owner is id // 32; one holder gives at most 2 ids to one owner, and in every stripe some owner receives 2 ids from every group.
All inputs are finite; a program needn't handle non-finite values.
Results may differ from a plain program's by a relative error of at most 0.000073.
Values sent between devices are 32-bit elements; how exact they have to be, the bound alone decides.
A program may use at most 64 MiB of HBM per device.

v0:
```python
import functools

import jax
import jax.numpy as jnp
from jax import lax
from jax.experimental import pallas as pl
from jax.experimental.pallas import tpu as pltpu
from jax.sharding import PartitionSpec as P

BPT = 8
PASSES = 4
NSEG = 4
MESH = pl.DeviceIdType.MESH

diffusion_rate = 0.0615


def halves(value):
    high = value.astype(jnp.bfloat16)
    return high, (value - high.astype(jnp.float32)).astype(jnp.bfloat16)


def product(left, right):
    left_high, left_low = halves(left)
    right_high, right_low = halves(right)
    dot = functools.partial(jnp.dot, preferred_element_type=jnp.float32)
    return dot(left_high, right_high) + (dot(left_high, right_low) + dot(left_low, right_high))


def kernel(
    n_ev, n_sp, ids_in, levels_in, blocks_in, smoother_in, scale_in, out,
    ids, levels, blocks, smoother, scale,
    outgoing, label_out, arrived, labels, here, there, beside_here, beside_there, coef, beside_coef,
    load_sem, send_sem, recv_sem, label_send_sem, label_recv_sem,
    label_pass_send_sem, label_pass_recv_sem,
):
    ev, sp = lax.axis_index("ev"), lax.axis_index("sp")
    rows, shells, width = coef.shape
    listed = blocks.shape[2]
    groups = recv_sem.shape[0]
    size = n_sp // groups

    loads = [
        pltpu.make_async_copy(given, held, load_sem.at[i])
        for i, (given, held) in enumerate(
            [(ids_in, ids), (blocks_in, blocks), (smoother_in, smoother), (levels_in, levels), (scale_in, scale)]
        )
    ]
    for load in loads:
        load.start()

    def holder(step):
        return lax.rem(sp + step, n_sp)

    def peer(step):
        return lax.rem(ev + step, n_ev)

    barrier = pltpu.get_barrier_semaphore()

    def greet(turn, step, carry):
        pl.semaphore_signal(barrier, inc=1, device_id=(peer(turn), holder(step)), device_id_type=MESH)
        return carry

    for turn in range(n_ev):
        lax.fori_loop(int(turn == 0), n_sp, functools.partial(greet, turn), 0)

    for load in loads[:3]:
        load.wait()
    columns = []
    for j in range(listed):
        block_id = ids[0, j]
        label_out[j : j + 1, :] = jnp.full((1, width), block_id // NSEG, jnp.int32)
        segment = lax.rem(block_id, NSEG)
        block = blocks[0, :, j, :]
        columns.append(
            jnp.concatenate([block * (segment == q).astype(jnp.float32) for q in range(NSEG)], axis=0)
        )
    smooth = product(smoother[...], jnp.concatenate(columns, axis=1))
    for m in range(n_sp):
        for j in range(listed):
            outgoing[m, j * shells : (j + 1) * shells, :] = smooth[
                m * shells : (m + 1) * shells, j * width : (j + 1) * width
            ]

    pl.semaphore_wait(barrier, n_sp * n_ev - 1)

    def label_copy(step):
        return pltpu.make_async_remote_copy(
            src_ref=label_out, dst_ref=labels.at[0, step], send_sem=label_send_sem,
            recv_sem=label_recv_sem, device_id=(ev, holder(step)), device_id_type=MESH,
        )

    def copy(step, turn):
        return pltpu.make_async_remote_copy(
            src_ref=outgoing.at[holder(step)], dst_ref=arrived.at[step * n_ev + turn], send_sem=send_sem,
            recv_sem=recv_sem.at[step // size], device_id=(peer(turn), holder(step)), device_id_type=MESH,
        )

    def send_label(step, carry):
        label_copy(step).start()
        return carry

    def send(step, carry):
        for turn in range(n_ev):
            copy(step, turn).start()
        return carry

    for turn in range(1, n_ev):
        copy(0, turn).start()
    lax.fori_loop(1, size, send, 0)
    lax.fori_loop(1, n_sp, send_label, 0)
    lax.fori_loop(size, n_sp, send, 0)

    arrived[0] = outgoing[sp]
    labels[0, 0] = label_out[...]

    for load in loads[3:]:
        load.wait()
    shell_of = lax.broadcasted_iota(jnp.int32, (shells, width), 0)
    level = jnp.zeros((shells, width), jnp.float32)
    for r in range(shells):
        level = jnp.where(shell_of == r, levels[r].astype(jnp.float32), level)
    level = diffusion_rate * level
    lane = lax.broadcasted_iota(jnp.int32, (1, width), 1)
    right_half = lane < width // 2
    after = jnp.minimum(ev + 1, n_ev - 1)
    before = jnp.maximum(ev - 1, 0)
    inside = jnp.where(right_half, (ev + 1 < n_ev).astype(jnp.float32), (ev > 0).astype(jnp.float32))

    def tile(start, which):
        return scale[pl.ds(start, BPT), pl.ds(pl.multiple_of(which * width, width), width)]

    def coefficients(stripe, carry):
        start = pl.multiple_of(stripe * BPT, BPT)
        main = tile(start, ev)
        sides = jnp.where(right_half, tile(start, after), tile(start, before)) * inside
        coef[pl.ds(start, BPT)] = level[None] * main[:, None, :]
        beside_coef[pl.ds(start, BPT)] = level[None] * sides[:, None, :]
        return carry

    lax.fori_loop(0, n_sp, coefficients, 0)
    blank = jnp.zeros((1, shells, width), jnp.float32)
    for field in (here, there, beside_here, beside_there):
        field[0:1] = blank
        field[rows + 1 : rows + 2] = blank

    def taken(buffer, one, two, step):
        return pltpu.make_async_remote_copy(
            src_ref=buffer, dst_ref=buffer, send_sem=one, recv_sem=two,
            device_id=(peer(step), sp), device_id_type=MESH,
        )

    def label_passed(step):
        return pltpu.make_async_remote_copy(
            src_ref=labels.at[0], dst_ref=labels.at[step],
            send_sem=label_pass_send_sem.at[step], recv_sem=label_pass_recv_sem.at[step],
            device_id=(peer(step), sp), device_id_type=MESH,
        )

    side_tile = jnp.where(right_half, ev + 1, ev - 1) * BPT

    def place(slot, carry):
        start = lax.rem(sp - slot + n_sp, n_sp) * BPT + 1
        main = [jnp.zeros((shells, width), jnp.float32) for _ in range(BPT)]
        sides = list(main)
        for turn in range(n_ev):
            for j in range(listed):
                block = arrived[slot * n_ev + turn, j * shells : (j + 1) * shells, :]
                label = jnp.broadcast_to(labels[turn, slot, j : j + 1, :], (shells, width))
                in_main = label - ev * BPT
                in_sides = label - side_tile
                for k in range(BPT):
                    main[k] = main[k] + jnp.where(in_main == k, block, 0.0)
                    sides[k] = sides[k] + jnp.where(in_sides == k, block, 0.0)
        for k in range(BPT):
            here[start + k] = main[k]
            beside_here[start + k] = sides[k]
        return carry

    label_span = labels.at[0, pl.ds(0, n_sp - 1)]
    taken(label_span, label_send_sem, label_recv_sem, 1).wait_recv()
    for step in range(1, n_ev):
        label_passed(step).start()
    for group in range(groups):
        count = size * n_ev - (group == 0)
        taken(arrived.at[pl.ds(0, count)], send_sem, recv_sem.at[group], 1).wait_recv()
        if group == 0:
            for step in range(1, n_ev):
                label_passed(step).wait_recv()
        lax.fori_loop(group * size, (group + 1) * size, place, 0, unroll=2)

    at_end = (lane == width - 1)[None]
    at_start = (lane == 0)[None]

    def diffuse(field, side_field, new_field, new_side):
        def chunk(stripe, carry):
            start = stripe * BPT
            main_rows = field[pl.ds(start, BPT + 2)]
            side_rows = side_field[pl.ds(start, BPT + 2)]
            main, sides = main_rows[1:-1], side_rows[1:-1]
            main_up, sides_up = pltpu.roll(main, width - 1, 2), pltpu.roll(sides, width - 1, 2)
            main_down, sides_down = pltpu.roll(main, 1, 2), pltpu.roll(sides, 1, 2)
            around = (
                main_rows[2:] + main_rows[:-2]
                + jnp.where(at_end, sides_up, main_up)
                + jnp.where(at_start, sides_down, main_down)
            )
            new = main + coef[pl.ds(start, BPT)] * (around - 4.0 * main)
            if new_field is None:
                out[pl.ds(start, BPT)] = new
                return carry
            new_field[pl.ds(start + 1, BPT)] = new
            around = (
                side_rows[2:] + side_rows[:-2]
                + jnp.where(at_end, main_up, sides_up)
                + jnp.where(at_start, main_down, sides_down)
            )
            new_side[pl.ds(start + 1, BPT)] = sides + beside_coef[pl.ds(start, BPT)] * (around - 4.0 * sides)
            return carry

        return chunk

    now, later = (here, beside_here), (there, beside_there)
    for repeat in range(PASSES - 1):
        lax.fori_loop(0, n_sp, diffuse(*now, *later), 0, unroll=4)
        now, later = later, now
    lax.fori_loop(0, n_sp, diffuse(*now, None, None), 0, unroll=4)

    taken(label_span, label_send_sem, label_recv_sem, 1).wait_send()
    for step in range(1, n_ev):
        label_passed(step).wait_send()
    taken(arrived.at[pl.ds(0, n_sp * n_ev - 1)], send_sem, recv_sem.at[0], 1).wait_send()


def solution(mesh):
    n_ev, n_sp = mesh.shape["ev"], mesh.shape["sp"]
    groups = 4

    def per_device(partial_kernels, block_ids, radial_smoother, shell_level, lateral_scale):
        listed, width = partial_kernels.shape[2:]
        shells = shell_level.shape[0]
        rows = lateral_scale.shape[0]
        field = pltpu.VMEM((rows + 2, shells, width), jnp.float32)
        inner = pltpu.VMEM((rows, shells, width), jnp.float32)
        given = (block_ids, shell_level, partial_kernels, radial_smoother, lateral_scale)
        dma = pltpu.SemaphoreType.DMA
        out = pl.pallas_call(
            functools.partial(kernel, n_ev, n_sp),
            out_shape=jax.ShapeDtypeStruct((rows, shells, width), jnp.float32),
            in_specs=[pl.BlockSpec(memory_space=pltpu.HBM)] * 5,
            out_specs=pl.BlockSpec(memory_space=pltpu.VMEM),
            scratch_shapes=[
                pltpu.SMEM(block_ids.shape, jnp.int32),
                pltpu.SMEM(shell_level.shape, jnp.int32),
                pltpu.VMEM(partial_kernels.shape, jnp.float32),
                pltpu.VMEM(radial_smoother.shape, jnp.float32),
                pltpu.VMEM(lateral_scale.shape, jnp.float32),
                pltpu.VMEM((n_sp, listed * shells, width), jnp.float32),
                pltpu.VMEM((listed, width), jnp.int32),
                pltpu.VMEM((n_sp * n_ev, listed * shells, width), jnp.float32),
                pltpu.VMEM((n_ev, n_sp, listed, width), jnp.int32),
                field, field, field, field, inner, inner,
                dma((5,)), dma, dma((groups,)), dma, dma, dma((n_ev,)), dma((n_ev,)),
            ],
            compiler_params=pltpu.CompilerParams(
                collective_id=0, has_side_effects=True, vmem_limit_bytes=40 * 1024 * 1024
            ),
        )(*[pltpu.with_memory_space_constraint(x, pltpu.HBM) for x in given])
        return jnp.transpose(out, (1, 0, 2))

    placed = (P("ev", None, "sp", None), P("ev", "sp"), P(), P("sp"), P())
    return jax.shard_map(
        per_device, mesh=mesh, in_specs=placed, out_specs=P("sp", None, "ev"), check_vma=False
    )
```

profile of v0, /device:TPU:0, one launch (start us, length us, event | category | flops | bytes accessed | tf_op | source)
XLA Modules:
  0.0 17.8 jit_solution(15759722116988535535)
XLA Ops:
  0.0 16.9 %shard_map.55 = f32[128,8,128]{2,1,0:T(8,128)S(1)} custom-call(s32[1,2]{1,0:T(1,128)} %ids_in.1, s32[8]{0:T(128)} %levels_in.1, f32[1,32,2,128]{3,2,1,0:T(2,128)} %blocks_in.1, f32[128,128]{1,0:T(8,128)} %smoother_in.1, f32[128,256]{1,0:T(8,128)} %scale_in.1), custom_call_target="tpu_custom_call" | custom-call | tf_op jit(solution)/shard_map/pallas_call | solution.py:247
  16.9 0.9 %copy.6 = f32[8,128,128]{2,1,0:T(8,128)} copy(f32[8,128,128]{2,0,1:T(8,128)S(1)} %bitcast.1) | data formatting | bytes 1048576 | tf_op jit(solution)/shard_map/transpose | solution.py:269
where the time goes:
time: 17.9 us; the launch traced here: 17.8 us
  Pallas kernels  16.9 us (94%)
  local copies, waits for them, and re-layouts  0.89 us (5%)
    pallas_call x1, Pallas kernels, per_device(): pl.pallas_call(functools.partial(kernel, n_ev, n_sp), out_shape=jax.Shape...  16.9 us
    transpose x1, local copies, waits for them, and re-layouts, per_device(): return jnp.transpose(out, (1, 0, 2))  0.89 us

commit v1 on v0

--- a/solution.py
+++ b/solution.py
@@ -30,7 +30,7 @@
 def kernel(
     n_ev, n_sp, ids_in, levels_in, blocks_in, smoother_in, scale_in, out,
     ids, levels, blocks, smoother, scale,
-    outgoing, label_out, arrived, labels, here, there, beside_here, beside_there, coef, beside_coef,
+    outgoing, label_out, arrived, labels, here, there, coef, strip_coef, edges, edge_labels, ends,
     load_sem, send_sem, recv_sem, label_send_sem, label_recv_sem,
     label_pass_send_sem, label_pass_recv_sem,
 ):
@@ -38,6 +38,9 @@
     rows, shells, width = coef.shape
     listed = blocks.shape[2]
     groups = recv_sem.shape[0]
+    sets = edges.shape[0]
+    span = 2 * PASSES
+    per_set = width // span
     size = n_sp // groups
 
     loads = [
@@ -122,25 +125,39 @@
         level = jnp.where(shell_of == r, levels[r].astype(jnp.float32), level)
     level = diffusion_rate * level
     lane = lax.broadcasted_iota(jnp.int32, (1, width), 1)
-    right_half = lane < width // 2
+    spot = lane & (span - 1)
+    group_of = lax.shift_right_logical(lane, span.bit_length() - 1)
+    late_half = lane >= width // 2
     after = jnp.minimum(ev + 1, n_ev - 1)
     before = jnp.maximum(ev - 1, 0)
-    inside = jnp.where(right_half, (ev + 1 < n_ev).astype(jnp.float32), (ev > 0).astype(jnp.float32))
+    has_after = (ev + 1 < n_ev).astype(jnp.float32)
+    has_before = (ev > 0).astype(jnp.float32)
 
     def tile(start, which):
         return scale[pl.ds(start, BPT), pl.ds(pl.multiple_of(which * width, width), width)]
 
-    def coefficients(stripe, carry):
-        start = pl.multiple_of(stripe * BPT, BPT)
+    left_scale = [jnp.zeros((BPT, width), jnp.float32)] * sets
+    right_scale = list(left_scale)
+    for stripe in range(n_sp):
+        start = stripe * BPT
         main = tile(start, ev)
-        sides = jnp.where(right_half, tile(start, after), tile(start, before)) * inside
         coef[pl.ds(start, BPT)] = level[None] * main[:, None, :]
-        beside_coef[pl.ds(start, BPT)] = level[None] * sides[:, None, :]
-        return carry
-
-    lax.fori_loop(0, n_sp, coefficients, 0)
+        which, local = divmod(stripe, per_set)
+        shift = (local * span + PASSES) % width
+        left = jnp.where(late_half, tile(start, before) * has_before, main)
+        right = jnp.where(late_half, main, tile(start, after) * has_after)
+        mine = group_of == local
+        left_scale[which] = jnp.where(mine, pltpu.roll(left, shift, 1), left_scale[which])
+        right_scale[which] = jnp.where(mine, pltpu.roll(right, shift, 1), right_scale[which])
+    for which in range(sets):
+        strip_coef[0, which] = level[None] * left_scale[which][:, None, :]
+        strip_coef[1, which] = level[None] * right_scale[which][:, None, :]
+        for entry in range(n_ev * listed):
+            edges[which, entry] = jnp.zeros((shells, width), jnp.float32)
+            edge_labels[which, entry] = jnp.full((shells, width), -n_ev * n_sp * BPT * span, jnp.int32)
+
     blank = jnp.zeros((1, shells, width), jnp.float32)
-    for field in (here, there, beside_here, beside_there):
+    for field in (here, there):
         field[0:1] = blank
         field[rows + 1 : rows + 2] = blank
 
@@ -157,24 +174,25 @@
             device_id=(peer(step), sp), device_id_type=MESH,
         )
 
-    side_tile = jnp.where(right_half, ev + 1, ev - 1) * BPT
-
     def place(slot, carry):
-        start = lax.rem(sp - slot + n_sp, n_sp) * BPT + 1
+        stripe = lax.rem(sp - slot + n_sp, n_sp)
+        start = stripe * BPT + 1
+        which, local = stripe // per_set, lax.rem(stripe, per_set)
+        shift = lax.rem(local * span + PASSES, width)
+        mine = group_of == local
         main = [jnp.zeros((shells, width), jnp.float32) for _ in range(BPT)]
-        sides = list(main)
         for turn in range(n_ev):
             for j in range(listed):
                 block = arrived[slot * n_ev + turn, j * shells : (j + 1) * shells, :]
                 label = jnp.broadcast_to(labels[turn, slot, j : j + 1, :], (shells, width))
+                entry = turn * listed + j
+                edges[which, entry] = jnp.where(mine, pltpu.roll(block, shift, 1), edges[which, entry])
+                edge_labels[which, entry] = jnp.where(mine, label, edge_labels[which, entry])
                 in_main = label - ev * BPT
-                in_sides = label - side_tile
                 for k in range(BPT):
                     main[k] = main[k] + jnp.where(in_main == k, block, 0.0)
-                    sides[k] = sides[k] + jnp.where(in_sides == k, block, 0.0)
         for k in range(BPT):
             here[start + k] = main[k]
-            beside_here[start + k] = sides[k]
         return carry
 
     label_span = labels.at[0, pl.ds(0, n_sp - 1)]
@@ -189,42 +207,78 @@
                 label_passed(step).wait_recv()
         lax.fori_loop(group * size, (group + 1) * size, place, 0, unroll=2)
 
+    def strip_of(inner, outer):
+        base = jnp.where(spot < PASSES, inner, outer) * BPT
+        strip = []
+        for which in range(sets):
+            found = [edge_labels[which, entry] - base for entry in range(n_ev * listed)]
+            values = [edges[which, entry] for entry in range(n_ev * listed)]
+            strip.append([
+                sum(jnp.where(at == k, value, 0.0) for at, value in zip(found, values)) for k in range(BPT)
+            ])
+        return strip
+
+    def across(strip, which, back):
+        k, far = (BPT - 1, 0) if back else (0, per_set - 1)
+        shift = span if back else width - span
+        beyond = which - 1 if back else which + 1
+        rolled = pltpu.roll(strip[which][k], shift, 1)
+        outside = pltpu.roll(strip[beyond][k], shift, 1) if 0 <= beyond < sets else 0.0
+        return jnp.where(group_of == far, outside, rolled)
+
+    def strip_pass(strip, side):
+        new = []
+        for which in range(sets):
+            new.append([])
+            for k in range(BPT):
+                cell = strip[which][k]
+                up = strip[which][k + 1] if k < BPT - 1 else across(strip, which, False)
+                down = strip[which][k - 1] if k > 0 else across(strip, which, True)
+                around = up + down + pltpu.roll(cell, width - 1, 1) + pltpu.roll(cell, 1, 1)
+                new[which].append(cell + strip_coef[side, which, k] * (around - 4.0 * cell))
+        return new
+
+    left, right = strip_of(ev - 1, ev), strip_of(ev, ev + 1)
+    for repeat in range(PASSES):
+        for which in range(sets):
+            for k in range(BPT):
+                ends[repeat, which, k] = jnp.where(
+                    spot == 0,
+                    pltpu.roll(left[which][k], width - PASSES + 1, 1),
+                    pltpu.roll(right[which][k], width - PASSES - 1, 1),
+                )
+        if repeat < PASSES - 1:
+            left, right = strip_pass(left, 0), strip_pass(right, 1)
+
     at_end = (lane == width - 1)[None]
     at_start = (lane == 0)[None]
 
-    def diffuse(field, side_field, new_field, new_side):
+    def diffuse(repeat, field, new_field):
         def chunk(stripe, carry):
             start = stripe * BPT
             main_rows = field[pl.ds(start, BPT + 2)]
-            side_rows = side_field[pl.ds(start, BPT + 2)]
-            main, sides = main_rows[1:-1], side_rows[1:-1]
-            main_up, sides_up = pltpu.roll(main, width - 1, 2), pltpu.roll(sides, width - 1, 2)
-            main_down, sides_down = pltpu.roll(main, 1, 2), pltpu.roll(sides, 1, 2)
+            main = main_rows[1:-1]
+            shift = lax.rem(width - lax.rem(stripe, per_set) * span, width)
+            outside = pltpu.roll(ends[repeat, stripe // per_set], shift, 2)
             around = (
                 main_rows[2:] + main_rows[:-2]
-                + jnp.where(at_end, sides_up, main_up)
-                + jnp.where(at_start, sides_down, main_down)
+                + jnp.where(at_end, outside, pltpu.roll(main, width - 1, 2))
+                + jnp.where(at_start, outside, pltpu.roll(main, 1, 2))
             )
             new = main + coef[pl.ds(start, BPT)] * (around - 4.0 * main)
             if new_field is None:
                 out[pl.ds(start, BPT)] = new
-                return carry
-            new_field[pl.ds(start + 1, BPT)] = new
-            around = (
-                side_rows[2:] + side_rows[:-2]
-                + jnp.where(at_end, main_up, sides_up)
-                + jnp.where(at_start, main_down, sides_down)
-            )
-            new_side[pl.ds(start + 1, BPT)] = sides + beside_coef[pl.ds(start, BPT)] * (around - 4.0 * sides)
+            else:
+                new_field[pl.ds(start + 1, BPT)] = new
             return carry
 
         return chunk
 
-    now, later = (here, beside_here), (there, beside_there)
-    for repeat in range(PASSES - 1):
-        lax.fori_loop(0, n_sp, diffuse(*now, *later), 0, unroll=4)
+    now, later = here, there
+    for repeat in range(PASSES):
+        last = repeat == PASSES - 1
+        lax.fori_loop(0, n_sp, diffuse(repeat, now, None if last else later), 0, unroll=4)
         now, later = later, now
-    lax.fori_loop(0, n_sp, diffuse(*now, None, None), 0, unroll=4)
 
     taken(label_span, label_send_sem, label_recv_sem, 1).wait_send()
     for step in range(1, n_ev):
@@ -240,6 +294,7 @@
         listed, width = partial_kernels.shape[2:]
         shells = shell_level.shape[0]
         rows = lateral_scale.shape[0]
+        sets = n_sp // (width // (2 * PASSES))
         field = pltpu.VMEM((rows + 2, shells, width), jnp.float32)
         inner = pltpu.VMEM((rows, shells, width), jnp.float32)
         given = (block_ids, shell_level, partial_kernels, radial_smoother, lateral_scale)
@@ -259,7 +314,11 @@
                 pltpu.VMEM((listed, width), jnp.int32),
                 pltpu.VMEM((n_sp * n_ev, listed * shells, width), jnp.float32),
                 pltpu.VMEM((n_ev, n_sp, listed, width), jnp.int32),
-                field, field, field, field, inner, inner,
+                field, field, inner,
+                pltpu.VMEM((2, sets, BPT, shells, width), jnp.float32),
+                pltpu.VMEM((sets, n_ev * listed, shells, width), jnp.float32),
+                pltpu.VMEM((sets, n_ev * listed, shells, width), jnp.int32),
+                pltpu.VMEM((PASSES, sets, BPT, shells, width), jnp.float32),
                 dma((5,)), dma, dma((groups,)), dma, dma, dma((n_ev,)), dma((n_ev,)),
             ],
             compiler_params=pltpu.CompilerParams(

time: 17.9 us -> 18.1 us (1.011)
  no operation moved by 1% of the time
where the time goes in v1:
time: 18.1 us; the launch traced here: 17.9 us
  Pallas kernels  17 us (94%)
  local copies, waits for them, and re-layouts  0.89 us (5%)
    pallas_call x1, Pallas kernels, per_device(): pl.pallas_call(functools.partial(kernel, n_ev, n_sp), out_shape=jax.Shape...  17 us
    transpose x1, local copies, waits for them, and re-layouts, per_device(): return jnp.transpose(out, (1, 0, 2))  0.89 us

profile of v1, /device:TPU:0, one launch (start us, length us, event | category | flops | bytes accessed | tf_op | source)
XLA Modules:
  0.0 17.9 jit_solution(5963022635126344700)
XLA Ops:
  0.0 17.0 %shard_map.55 = f32[128,8,128]{2,1,0:T(8,128)S(1)} custom-call(s32[1,2]{1,0:T(1,128)} %ids_in.1, s32[8]{0:T(128)} %levels_in.1, f32[1,32,2,128]{3,2,1,0:T(2,128)} %blocks_in.1, f32[128,128]{1,0:T(8,128)} %smoother_in.1, f32[128,256]{1,0:T(8,128)} %scale_in.1), custom_call_target="tpu_custom_call" | custom-call | tf_op jit(solution)/shard_map/pallas_call | solution.py:302
  17.0 0.9 %copy.6 = f32[8,128,128]{2,1,0:T(8,128)} copy(f32[8,128,128]{2,0,1:T(8,128)S(1)} %bitcast.1) | data formatting | bytes 1048576 | tf_op jit(solution)/shard_map/transpose | solution.py:328

commit v2 on v1

--- a/solution.py
+++ b/solution.py
@@ -37,11 +37,11 @@
     ev, sp = lax.axis_index("ev"), lax.axis_index("sp")
     rows, shells, width = coef.shape
     listed = blocks.shape[2]
-    groups = recv_sem.shape[0]
+    size = recv_sem.shape[0]
+    groups = n_sp // size
     sets = edges.shape[0]
     span = 2 * PASSES
     per_set = width // span
-    size = n_sp // groups
 
     loads = [
         pltpu.make_async_copy(given, held, load_sem.at[i])
@@ -96,23 +96,26 @@
     def copy(step, turn):
         return pltpu.make_async_remote_copy(
             src_ref=outgoing.at[holder(step)], dst_ref=arrived.at[step * n_ev + turn], send_sem=send_sem,
-            recv_sem=recv_sem.at[step // size], device_id=(peer(turn), holder(step)), device_id_type=MESH,
+            recv_sem=recv_sem.at[lax.rem(step, size)], device_id=(peer(turn), holder(step)), device_id_type=MESH,
         )
 
     def send_label(step, carry):
         label_copy(step).start()
         return carry
 
-    def send(step, carry):
-        for turn in range(n_ev):
-            copy(step, turn).start()
+    order = [*range(groups // 2, groups), *range(groups // 2)]
+
+    def send(turn_of, carry):
+        for quarter in order:
+            for turn in range(n_ev):
+                copy(quarter * size + turn_of, turn).start()
         return carry
 
-    for turn in range(1, n_ev):
-        copy(0, turn).start()
+    lax.fori_loop(1, n_sp, send_label, 0)
+    for quarter in order:
+        for turn in range(int(quarter == 0), n_ev):
+            copy(jnp.int32(quarter * size), turn).start()
     lax.fori_loop(1, size, send, 0)
-    lax.fori_loop(1, n_sp, send_label, 0)
-    lax.fori_loop(size, n_sp, send, 0)
 
     arrived[0] = outgoing[sp]
     labels[0, 0] = label_out[...]
@@ -174,7 +177,8 @@
             device_id=(peer(step), sp), device_id_type=MESH,
         )
 
-    def place(slot, carry):
+    def place(group, quarter, carry):
+        slot = quarter * size + group
         stripe = lax.rem(sp - slot + n_sp, n_sp)
         start = stripe * BPT + 1
         which, local = stripe // per_set, lax.rem(stripe, per_set)
@@ -199,13 +203,13 @@
     taken(label_span, label_send_sem, label_recv_sem, 1).wait_recv()
     for step in range(1, n_ev):
         label_passed(step).start()
-    for group in range(groups):
-        count = size * n_ev - (group == 0)
+    for group in range(size):
+        count = groups * n_ev - (group == 0)
         taken(arrived.at[pl.ds(0, count)], send_sem, recv_sem.at[group], 1).wait_recv()
         if group == 0:
             for step in range(1, n_ev):
                 label_passed(step).wait_recv()
-        lax.fori_loop(group * size, (group + 1) * size, place, 0, unroll=2)
+        lax.fori_loop(0, groups, functools.partial(place, group), 0, unroll=2)
 
     def strip_of(inner, outer):
         base = jnp.where(spot < PASSES, inner, outer) * BPT
@@ -319,7 +323,7 @@
                 pltpu.VMEM((sets, n_ev * listed, shells, width), jnp.float32),
                 pltpu.VMEM((sets, n_ev * listed, shells, width), jnp.int32),
                 pltpu.VMEM((PASSES, sets, BPT, shells, width), jnp.float32),
-                dma((5,)), dma, dma((groups,)), dma, dma, dma((n_ev,)), dma((n_ev,)),
+                dma((5,)), dma, dma((n_sp // groups,)), dma, dma, dma((n_ev,)), dma((n_ev,)),
             ],
             compiler_params=pltpu.CompilerParams(
                 collective_id=0, has_side_effects=True, vmem_limit_bytes=40 * 1024 * 1024

time: 18.1 us -> 19.1 us (1.055)
  Pallas kernels: 17 us -> 18.1 us
    pallas_call x1, Pallas kernels: 17 us -> 18.1 us  [per_device(): pl.pallas_call(functools.partial(kernel, n_ev, n_sp), out_shape=jax.Shape...]
where the time goes in v2:
time: 19.1 us; the launch traced here: 19 us
  Pallas kernels  18.1 us (95%)
  local copies, waits for them, and re-layouts  0.89 us (5%)
    pallas_call x1, Pallas kernels, per_device(): pl.pallas_call(functools.partial(kernel, n_ev, n_sp), out_shape=jax.Shape...  18.1 us
    transpose x1, local copies, waits for them, and re-layouts, per_device(): return jnp.transpose(out, (1, 0, 2))  0.89 us

profile of v2, /device:TPU:0, one launch (start us, length us, event | category | flops | bytes accessed | tf_op | source)
XLA Modules:
  0.0 19.0 jit_solution(13632715320528329452)
XLA Ops:
  0.0 18.1 %shard_map.55 = f32[128,8,128]{2,1,0:T(8,128)S(1)} custom-call(s32[1,2]{1,0:T(1,128)} %ids_in.1, s32[8]{0:T(128)} %levels_in.1, f32[1,32,2,128]{3,2,1,0:T(2,128)} %blocks_in.1, f32[128,128]{1,0:T(8,128)} %smoother_in.1, f32[128,256]{1,0:T(8,128)} %scale_in.1), custom_call_target="tpu_custom_call" | custom-call | tf_op jit(solution)/shard_map/pallas_call | solution.py:306
  18.1 0.9 %copy.6 = f32[8,128,128]{2,1,0:T(8,128)} copy(f32[8,128,128]{2,0,1:T(8,128)S(1)} %bitcast.1) | data formatting | bytes 1048576 | tf_op jit(solution)/shard_map/transpose | solution.py:332
